TPU v7x, 32 devices: a whole 2x2x4 slice. The times are simulated.
32 devices in a mesh: group: 2 (over x), fsdp: 8 (over z, y), dp: 2 (over core).
Axes of the slice: x: 2, y: 2, z: 4, core: 2. Of those that a mesh axis runs over, the one named last changes fastest.
Arguments:
- hidden: bfloat16 [2048, 28672], P(('group', 'dp'), 'fsdp'), parts along dimension 0, may hold values from -6 to 6
- cotangent: bfloat16 [2048, 8192], P(('group', 'dp'), 'fsdp'), parts along dimension 0, may hold values from -6 to 6
- down_weight: bfloat16 [28672, 8192], P('fsdp', 'dp'), may hold values from -0.0625 to 0.0625
- proj_in: bfloat16 [28672, 128], P('fsdp'), may hold values from -0.03125 to 0.03125
- proj_out: bfloat16 [8192, 64], replicated, may hold values from -0.0625 to 0.0625
- valid_proj: bfloat16 [2048, 8192], P(('group', 'fsdp')), parts along dimension 0, may hold values from -0.00390625 to 0.00390625
- lengths: int32 [8], P(('group', 'dp')), parts along dimension 0, may hold values from 64 to 256
Outputs:
- hidden_grad: bfloat16 [2048, 28672], P(('group', 'dp'), 'fsdp'), parts along dimension 0
- scores: float32 [8, 1024], P(('group', 'dp'), 'fsdp'), parts along dimension 0
There are 2 independent parts, one for each index of `group`. A program takes and returns all parts, laid end to end along the dimension named above; an argument that names none is the same for every part. Nothing has to cross between parts.
All inputs are finite; a program needn't handle non-finite values.
Results may differ from a plain program's by a relative error of at most 0.0029.
Values may be sent and summed in bfloat16 or wider, within the bound.
A program may use at most 256 MiB of HBM per device.

v0:
```python
import jax
import jax.numpy as jnp
from jax import lax
from jax.sharding import PartitionSpec as P

K_IN = 128
K_OUT = 64
SEQ = 256


def outer_sum(outs, acts):
    count = outs.shape[0] // SEQ
    grads = jnp.einsum(
        "etk,etj->ekj",
        outs.reshape(count, SEQ, K_OUT),
        acts.reshape(count, SEQ, K_IN),
        precision=lax.Precision.HIGHEST,
    )
    return grads.reshape(count, K_OUT * K_IN)


def per_device(hidden, cotangent, down_weight, proj_in, proj_out, valid_proj, lengths):
    positions = jnp.arange(SEQ, dtype=jnp.int32)
    keep_mask = (positions[None, :] < lengths[:, None]).astype(jnp.bfloat16).reshape(-1, 1)
    masked = cotangent * keep_mask
    gathered = lax.all_gather(masked, "fsdp", axis=1, tiled=True)
    hidden_grad = lax.dot_general(
        gathered,
        lax.all_gather(down_weight, "dp", axis=1, tiled=True),
        (((1,), (1,)), ((), ())),
        preferred_element_type=jnp.float32,
    ).astype(jnp.bfloat16)
    part_acts = jnp.dot(hidden, proj_in, preferred_element_type=jnp.float32)
    outs = jnp.dot(gathered, proj_out, preferred_element_type=jnp.float32)
    acts = lax.psum(part_acts, "fsdp")
    grads = outer_sum(outs, acts)
    grads_low = grads.astype(jnp.bfloat16)
    scores = lax.dot_general(
        grads_low, valid_proj, (((1,), (1,)), ((), ())), preferred_element_type=jnp.float32
    )
    return (hidden_grad, scores)


def solution(mesh):
    in_specs = (
        P(("group", "dp"), "fsdp"),
        P(("group", "dp"), "fsdp"),
        P("fsdp", "dp"),
        P("fsdp", None),
        P(),
        P(("group", "fsdp"), None),
        P(("group", "dp")),
    )
    out_specs = (P(("group", "dp"), "fsdp"), P(("group", "dp"), "fsdp"))
    return jax.shard_map(
        per_device, mesh=mesh, in_specs=in_specs, out_specs=out_specs, check_vma=False
    )
```

profile of v0, /device:TPU:19, one launch (start us, length us, event | category | flops | bytes accessed | tf_op | source)
XLA Modules:
  0.0 339.7 jit_solution(8289953298900246120)
XLA Ops:
  7.2 0.0 copy-start
  7.2 0.0 all-gather.3.cloned.1.call-start
  7.2 0.9 fusion.6
  8.1 2.3 broadcast_multiply_fusion
  10.4 0.0 all-gather.3.cloned.1.call-update
  10.5 0.0 all-reduce.2.cloned.1.call-start
  10.5 4.1 %fusion.8 = f32[512,128]{1,0:T(8,128)} fusion(bf16[512,3584]{1,0:T(8,128)(2,1)} %param.7, bf16[3584,128]{1,0:T(8,128)(2,1)} %param.10), kind=kOutput, calls=%fused_computation.12 | convolution fusion | flops 469762048 | bytes 4849664 | tf_op jit(solution)/shard_map/dot_general | solution.py:33
  14.6 0.0 all-reduce.2.cloned.1.call-update
  14.6 0.0 copy-start.2
  14.7 0.0 all-gather.5.cloned.1.call-start
  14.7 0.7 all-gather.5.cloned.1.call-update
  15.4 120.1 %all-gather.3.cloned.1.call-done = bf16[512,8192]{1,0:T(8,128)(2,1)} async-done(((bf16[512,1024]{1,0:T(8,128)(2,1)}), bf16[512,8192]{1,0:T(8,128)(2,1)}) %all-gather.3.cloned.1.call-update) | async-done | bytes 8388624 | tf_op jit(solution)/shard_map/all_gather | solution.py:26
  135.5 0.0 copy-done.2
  135.5 6.0 %fusion.7 = f32[512,64]{0,1:T(8,128)S(1)} fusion(bf16[512,8192]{1,0:T(8,128)(2,1)} %all-gather.3.cloned.1.call-done, bf16[8192,64]{0,1:T(8,128)(2,1)S(1)} %copy-done.2), kind=kOutput, calls=%fused_computation.11 | convolution fusion | flops 536870912 | bytes 9568256 | tf_op jit(solution)/shard_map/dot_general | solution.py:34
  141.5 64.7 %all-reduce.2.cloned.1.call-done = f32[2,256,128]{2,1,0:T(8,128)} async-done(((f32[2,256,128]{2,1,0:T(8,128)}), f32[2,256,128]{2,1,0:T(8,128)}) %all-reduce.2.cloned.1.call-update) | async-done | bytes 262160 | tf_op jit(solution)/shard_map/psum | solution.py:35
  206.2 1.2 fusion
  207.4 0.0 copy-done
  207.4 1.2 fusion.3
  208.7 86.1 %all-gather.5.cloned.1.call-done = bf16[3584,8192]{1,0:T(8,128)(2,1)} async-done(((bf16[3584,4096]{1,0:T(8,128)(2,1)}), bf16[3584,8192]{1,0:T(8,128)(2,1)}) %all-gather.5.cloned.1.call-update) | async-done | bytes 58720272 | tf_op jit(solution)/shard_map/all_gather | solution.py:29
  294.8 0.0 copy-start.1
  294.8 38.4 %convolution_convert_fusion = bf16[512,3584]{1,0:T(8,128)(2,1)} fusion(bf16[512,8192]{1,0:T(8,128)(2,1)} %all-gather.3.cloned.1.call-done, bf16[3584,8192]{1,0:T(8,128)(2,1)} %all-gather.5.cloned.1.call-done), kind=kOutput, calls=%fused_computation | convolution fusion | flops 30066606080 | bytes 70778880 | tf_op jit(solution)/shard_map/dot_general | solution.py:27
  333.2 0.0 copy-done.1
  (1 shorter events, 0.0 us)
Async XLA Ops:
  7.2 200.3 %copy-start = (bf16[128,8192]{1,0:T(8,128)(2,1)S(1)}, bf16[128,8192]{1,0:T(8,128)(2,1)}, u32[]{:S(2)}) copy-start(bf16[128,8192]{1,0:T(8,128)(2,1)} %param.12) | copy-start | bytes 6291460
  7.2 128.3 %all-gather.3.cloned.1.call-start = ((), (), s32[]{:S(2)}) async-start(), calls=%async_computation | async-start | bytes 9437184 | tf_op jit(solution)/shard_map/all_gather | solution.py:26
  10.5 195.7 %all-reduce.2.cloned.1.call-start = ((), (), s32[]{:S(2)}) async-start(), calls=%async_computation.2 | async-start | bytes 524288 | tf_op jit(solution)/shard_map/psum | solution.py:35
  14.6 120.8 %copy-start.2 = (bf16[8192,64]{0,1:T(8,128)(2,1)S(1)}, bf16[8192,64]{0,1:T(8,128)(2,1)}, u32[]{:S(2)}) copy-start(bf16[8192,64]{0,1:T(8,128)(2,1)} %param.11) | copy-start | bytes 3145732
  14.7 280.1 %all-gather.5.cloned.1.call-start = ((), (), s32[]{:S(2)}) async-start(), calls=%async_computation.1 | async-start | bytes 88080384 | tf_op jit(solution)/shard_map/all_gather | solution.py:29
  294.8 38.4 %copy-start.1 = (bf16[128,8192]{1,0:T(8,128)(2,1)S(1)}, bf16[128,8192]{1,0:T(8,128)(2,1)}, u32[]{:S(2)}) copy-start(bf16[128,8192]{1,0:T(8,128)(2,1)} %param.12) | copy-start | bytes 6291460
Sparse Core Ops, SparseCore 0:
  10.8 124.6 all-gather.2
  138.8 67.3 all-reduce.1
  207.8 86.8 all-gather.4
where the time goes:
time: 341 us; the launch traced here: 340 us
  waiting for transfers between devices  272 us (80%)
  matrix products  51 us (15%)
  between operations  13.8 us (4%)
    all_gather x1, waiting for transfers between devices, per_device(): gathered = lax.all_gather(masked, 'fsdp', axis=1, tiled=True)  120 us
    all_gather x1, waiting for transfers between devices, per_device(): lax.all_gather(down_weight, 'dp', axis=1, tiled=True)  86.1 us
    psum x1, waiting for transfers between devices, per_device(): acts = lax.psum(part_acts, 'fsdp')  64.7 us
    dot_general x1, matrix products, per_device(): lax.dot_general(gathered, lax.all_gather(down_weight, 'dp', axis=1, tiled...  38.4 us
  transfers between devices with their start and end apart: 3, of which 3 were waited for; matrix products, arithmetic and copies ran while one was open for 4% of the time, Pallas kernels for 0%

commit v1 on v0

v1 whole, which is shorter than its diff:
```python
import functools

import jax
import jax.numpy as jnp
from jax import lax
from jax.experimental import pallas as pl
from jax.experimental.pallas import tpu as pltpu
from jax.sharding import PartitionSpec as P

K_IN = 128
K_OUT = 64
SEQ = 256
TILES = 7
ROWS = 128


def kernel(
    F, snake,
    len_ref, hid, cot, w, pin, pout, out, grads,
    X, W, acc, inc, stage, own, po, pi, part, rA, gR,
    ld_sem, w_sem, sib_send, sib_recv, ring_send, ring_recv,
    rs_send, rs_recv, gs_send, gs_recv, ex_send, ex_recv, out_sem,
):
    f = lax.axis_index("fsdp")
    c = lax.axis_index("dp")
    H = F // 2
    T, Dl = own.shape
    FFl = acc.shape[2]
    Tc = T // F
    tile = FFl // TILES

    if snake:
        y, z = lax.rem(f, 2), f // 2
        p = (1 - y) * z + y * (F - 1 - z)

        def at(q):
            h = q // H
            return (1 - h) * (2 * q) + h * (2 * F - 1 - 2 * q)
    else:
        p = f

        def at(q):
            return q

    targets = (at(lax.rem(p + 1, F)), at(lax.rem(p + F - 1, F)))

    def source(d, s):
        q = lax.rem(p - s + F, F) if d == 0 else lax.rem(p + s, F)
        src = at(q)
        half = src // H
        return src - half * H, 1 - (half + c - 2 * half * c)

    def rows(k):
        return pl.ds(k * SEQ, SEQ)

    def ring(slot, d, k):
        i = slot * 4 + d * 2 + k
        return pltpu.make_async_remote_copy(
            src_ref=X.at[slot, d, rows(k)],
            dst_ref=X.at[slot, d, rows(k)],
            send_sem=ring_send.at[i],
            recv_sem=ring_recv.at[i],
            device_id={"fsdp": targets[d]},
            device_id_type=pl.DeviceIdType.MESH,
        )

    def exchange(d, k):
        return pltpu.make_async_remote_copy(
            src_ref=acc.at[d, rows(k)],
            dst_ref=inc.at[rows(k)],
            send_sem=ex_send.at[k],
            recv_sem=ex_recv.at[k],
            device_id={"dp": 1 - c},
            device_id_type=pl.DeviceIdType.MESH,
        )

    my_half = f // H
    my_slot = f - my_half * H

    def sibling(d, k):
        return pltpu.make_async_remote_copy(
            src_ref=own.at[rows(k)],
            dst_ref=X.at[my_slot, d, rows(k)],
            send_sem=sib_send.at[k],
            recv_sem=sib_recv.at[k],
            device_id={"dp": 1 - c},
            device_id_type=pl.DeviceIdType.MESH,
        )

    load_cot = pltpu.make_async_copy(cot, own, ld_sem.at[0])
    load_cot.start()
    load_po = pltpu.make_async_copy(pout.at[pl.ds(f * Dl, Dl)], po, ld_sem.at[1])
    load_po.start()
    load_pi = pltpu.make_async_copy(pin, pi, ld_sem.at[2])
    load_pi.start()

    def load_hid(h):
        return pltpu.make_async_copy(
            hid.at[pl.ds(h * ROWS, ROWS)], stage.at[h % 2], ld_sem.at[3 + h % 2]
        )

    load_hid(0).start()
    load_hid(1).start()

    def load_w(i):
        return pltpu.make_async_copy(w.at[:, pl.ds(i * Dl, Dl)], W.at[i], w_sem.at[i])

    for i in range(H):
        load_w(i).start()

    barrier = pltpu.get_barrier_semaphore()

    @pl.loop(1, F)
    def _(j):
        pl.semaphore_signal(
            barrier, inc=1, device_id={"fsdp": lax.rem(f + j, F)},
            device_id_type=pl.DeviceIdType.MESH,
        )

    pl.semaphore_signal(
        barrier, inc=1, device_id={"dp": 1 - c}, device_id_type=pl.DeviceIdType.MESH
    )

    load_cot.wait()
    mine = my_half == c
    for k in range(2):
        position = lax.broadcasted_iota(jnp.int32, (SEQ, Dl), 0)
        block = own[rows(k), :]
        masked = jnp.where(position < len_ref[k], block.astype(jnp.float32), 0.0)
        own[rows(k), :] = masked.astype(block.dtype)
    pl.semaphore_wait(barrier, F)

    slot0, act0 = my_slot, 1 - (my_half + c - 2 * my_half * c)

    @pl.when(my_half != c)
    def _():
        for k in range(2):
            for d in range(2):
                @pl.when(c == d)
                def _():
                    sibling(d, k).start()

    @pl.when(mine)
    def _():
        for k in range(2):
            X[my_slot, c, rows(k), :] = own[rows(k), :]
        for d in range(2):
            @pl.when(c == d)
            def _():
                for k in range(2):
                    ring(my_slot, d, k).start()
        for d in range(2):
            @pl.when(c != d)
            def _():
                for k in range(2):
                    sibling(d, k).wait_recv()
                    ring(my_slot, d, k).start()

    load_po.wait()
    for k in range(2):
        o = jnp.dot(own[rows(k), :], po[...], preferred_element_type=jnp.float32)
        for j in range(SEQ // Tc):
            first = o[j * Tc : j * Tc + Tc // 2]
            second = o[j * Tc + Tc // 2 : (j + 1) * Tc]
            part[k * (SEQ // Tc) + j, Tc : Tc + Tc // 2, 0:K_OUT] = first
            part[k * (SEQ // Tc) + j, Tc : Tc + Tc // 2, K_OUT : 2 * K_OUT] = second
    load_pi.wait()
    for h in range(T // ROWS):
        load_hid(h).wait()
        a = jnp.dot(stage[h % 2], pi[...], preferred_element_type=jnp.float32)
        if h + 2 < T // ROWS:
            load_hid(h + 2).start()
        for j in range(ROWS // Tc):
            part[h * (ROWS // Tc) + j, 0:Tc, :] = a[j * Tc : (j + 1) * Tc]

    def scatter(t, src, dst):
        return pltpu.make_async_remote_copy(
            src_ref=part.at[src], dst_ref=rA.at[dst],
            send_sem=rs_send.at[t], recv_sem=rs_recv.at[dst],
            device_id={"fsdp": t}, device_id_type=pl.DeviceIdType.MESH,
        )

    def spread(t, dst):
        return pltpu.make_async_remote_copy(
            src_ref=gR.at[f], dst_ref=gR.at[dst],
            send_sem=gs_send.at[t], recv_sem=gs_recv.at[dst],
            device_id={"fsdp": t}, device_id_type=pl.DeviceIdType.MESH,
        )

    @pl.loop(1, F)
    def _(j):
        t = lax.rem(f + j, F)
        scatter(t, t, f).start()

    def reduce_acts():
        def add(j, total):
            t = lax.rem(f + j, F)
            scatter(t, t, t).wait_recv()
            return total + rA[t]

        total = lax.fori_loop(1, F, add, part[f])
        tn = (((0,), (0,)), ((), ()))
        g = jnp.zeros((K_OUT, K_IN), jnp.float32)
        for u in range(2):
            g = g + lax.dot_general(
                total[Tc : Tc + Tc // 2, u * K_OUT : (u + 1) * K_OUT],
                total[u * (Tc // 2) : (u + 1) * (Tc // 2), :],
                tn, precision=lax.Precision.HIGHEST,
                preferred_element_type=jnp.float32,
            )
        gR[f] = g

        @pl.loop(1, F)
        def _(j):
            t = lax.rem(f + j, F)
            spread(t, f).start()

    def reduce_grads():
        @pl.loop(1, F)
        def _(j):
            t = lax.rem(f + j, F)
            spread(t, t).wait_recv()

        for e in range(2):
            g = gR[e * H]
            for t in range(1, H):
                g = g + gR[e * H + t]
            grads[e] = g.astype(grads.dtype)

    def product(slot, d, k):
        block = X.at[slot, d, rows(k)]

        @pl.loop(0, TILES)
        def _(i):
            n = pl.ds(pl.multiple_of(i * tile, tile), tile)
            acc[d, rows(k), n] += lax.dot_general(
                block[...], W[slot, n, :], (((1,), (1,)), ((), ())),
                preferred_element_type=jnp.float32,
            )

    @pl.loop(0, T // 8)
    def _(i):
        r = pl.ds(pl.multiple_of(i * 8, 8), 8)
        for d in range(2):
            acc[d, r, :] = jnp.zeros((8, FFl), jnp.float32)

    for i in range(H):
        load_w(i).wait()

    @pl.when(mine)
    def _():
        for k in range(2):
            for d in range(2):
                product(my_slot, d, k)

    def step(s, counts):
        slots, acts, seen = [], [], []
        for d in range(2):
            slot, act = source(d, s)
            slots.append(slot)
            acts.append(act)
            seen.append(counts[d] + act)
        for k in range(2):
            for d in range(2):
                @pl.when(acts[d] == 1)
                def _():
                    ring(slots[d], d, k).wait_recv()

                    @pl.when(s < F - 1)
                    def _():
                        ring(slots[d], d, k).start()

            for d in range(2):
                @pl.when(acts[d] == 1)
                def _():
                    product(slots[d], d, k)

                    @pl.when(seen[d] == H)
                    def _():
                        @pl.when(c != d)
                        def _():
                            exchange(d, k).start()

        @pl.when(s == 3)
        def _():
            reduce_acts()

        @pl.when(s == 5)
        def _():
            reduce_grads()

        return tuple(seen)

    lax.fori_loop(1, F, step, (act0, act0))

    def write(b):
        return pltpu.make_async_copy(
            stage.at[b % 2], out.at[pl.ds(b * ROWS, ROWS)], out_sem.at[b % 2]
        )

    per = SEQ // ROWS
    for b in range(T // ROWS):
        if b % per == 0:
            exchange(0, b // per).wait_recv()
        if b >= 2:
            write(b - 2).wait()

        @pl.loop(0, ROWS // 16)
        def _(i):
            r = pl.ds(pl.multiple_of(b * ROWS + i * 16, 16), 16)
            o = pl.ds(pl.multiple_of(i * 16, 16), 16)
            stage[b % 2, o, :] = (acc[c, r, :] + inc[r, :]).astype(stage.dtype)

        write(b).start()

    for b in range(T // ROWS - 2, T // ROWS):
        write(b).wait()

    @pl.when(my_half != c)
    def _():
        for k in range(2):
            sibling(0, k).wait_send()

    for k in range(2):
        exchange(0, k).wait_send()

    @pl.loop(1, F)
    def _(j):
        t = lax.rem(f + j, F)
        scatter(t, t, f).wait_send()
        spread(t, f).wait_send()

    @pl.loop(0, F - 1)
    def _(s):
        for d in range(2):
            slot, act = source(d, s)

            @pl.when(act == 1)
            def _():
                for k in range(2):
                    ring(slot, d, k).wait_send()


def per_device(F, hidden, cotangent, down_weight, proj_in, proj_out, valid_proj, lengths):
    T, FFl = hidden.shape
    Dl = cotangent.shape[1]
    H = F // 2
    Tc = T // F
    any_spec = pl.BlockSpec(memory_space=pl.ANY)
    vmem = pl.BlockSpec(memory_space=pltpu.VMEM)
    dma = pltpu.SemaphoreType.DMA
    hidden_grad, grads_low = pl.pallas_call(
        functools.partial(kernel, F, F == 8),
        out_shape=(
            jax.ShapeDtypeStruct((T, FFl), jnp.bfloat16),
            jax.ShapeDtypeStruct((2, K_OUT, K_IN), jnp.bfloat16),
        ),
        in_specs=[pl.BlockSpec(memory_space=pltpu.SMEM)] + [any_spec] * 5,
        out_specs=(any_spec, vmem),
        scratch_shapes=[
            pltpu.VMEM((H, 2, T, Dl), jnp.bfloat16),
            pltpu.VMEM((H, FFl, Dl), jnp.bfloat16),
            pltpu.VMEM((2, T, FFl), jnp.float32),
            pltpu.VMEM((T, FFl), jnp.float32),
            pltpu.VMEM((2, ROWS, FFl), jnp.bfloat16),
            pltpu.VMEM((T, Dl), jnp.bfloat16),
            pltpu.VMEM((Dl, K_OUT), jnp.bfloat16),
            pltpu.VMEM((FFl, K_IN), jnp.bfloat16),
            pltpu.VMEM((F, Tc + Tc // 2, K_IN), jnp.float32),
            pltpu.VMEM((F, Tc + Tc // 2, K_IN), jnp.float32),
            pltpu.VMEM((F, K_OUT, K_IN), jnp.float32),
            dma((5,)), dma((H,)), dma((2,)), dma((2,)), dma((4 * H,)), dma((4 * H,)),
            dma((F,)), dma((F,)), dma((F,)), dma((F,)), dma((2,)), dma((2,)), dma((2,)),
        ],
        compiler_params=pltpu.CompilerParams(
            collective_id=0, has_side_effects=True, vmem_limit_bytes=66584576
        ),
    )(lengths, hidden, cotangent, down_weight, proj_in, proj_out)
    scores = lax.dot_general(
        grads_low.reshape(2, K_OUT * K_IN), valid_proj, (((1,), (1,)), ((), ())),
        preferred_element_type=jnp.float32,
    )
    return hidden_grad, scores


def solution(mesh):
    in_specs = (
        P(("group", "dp"), "fsdp"),
        P(("group", "dp"), "fsdp"),
        P("fsdp", "dp"),
        P("fsdp", None),
        P(),
        P(("group", "fsdp"), None),
        P(("group", "dp")),
    )
    out_specs = (P(("group", "dp"), "fsdp"), P(("group", "dp"), "fsdp"))
    return jax.shard_map(
        functools.partial(per_device, mesh.shape["fsdp"]),
        mesh=mesh, in_specs=in_specs, out_specs=out_specs, check_vma=False,
    )
```

time: 341 us -> 137 us (0.40)
  waiting for transfers between devices: 272 us -> 0 us
  Pallas kernels: 0 us -> 126 us
  matrix products: 51 us -> 2.83 us
  between operations: 13.8 us -> 0.64 us
  local copies, waits for them, and re-layouts: 0.03 us -> 6.83 us
    all_gather x2 -> x0, waiting for transfers between devices: 206 us -> none  [the longest x1 120 us: per_device(): gathered = lax.all_gather(masked, 'fsdp', axis=1, tiled=True)]
    pallas_call x0 -> x1, Pallas kernels: none -> 126 us  [per_device(): pl.pallas_call(functools.partial(kernel, F, F == 8), out_shape=(jax.Shape...]
    psum x1 -> x0, waiting for transfers between devices: 64.7 us -> none  [per_device(): acts = lax.psum(part_acts, 'fsdp')]
    dot_general x5 -> x1, matrix products: 51 us -> 2.83 us  [per_device(): lax.dot_general(grads_low.reshape(2, K_OUT * K_IN), valid_proj, (((1,), (...]
    unnamed x7 -> x2, local copies, waits for them, and re-layouts: 0.03 us -> 6.83 us
  transfers between devices with their start and end apart: 3 -> 0, of which waited for: 3 -> 0; matrix products, arithmetic and copies ran while one was open for 4% -> 0% of each run, Pallas kernels for 0% -> 0%
where the time goes in v1:
time: 137 us; the launch traced here: 136 us
  Pallas kernels  126 us (92%)
  local copies, waits for them, and re-layouts  6.83 us (5%)
  matrix products  2.83 us (2%)
    pallas_call x1, Pallas kernels, per_device(): pl.pallas_call(functools.partial(kernel, F, F == 8), out_shape=(jax.Shape...  126 us
    unnamed x2, local copies, waits for them, and re-layouts  6.83 us
    dot_general x1, matrix products, per_device(): lax.dot_general(grads_low.reshape(2, K_OUT * K_IN), valid_proj, (((1,), (...  2.83 us

profile of v1, /device:TPU:19, one launch (start us, length us, event | category | flops | bytes accessed | tf_op | source)
XLA Modules:
  0.0 136.5 jit_solution(10455447541583134396)
XLA Ops:
  0.6 2.7 %copy.9.pout = bf16[8192,64]{1,0:T(8,128)(2,1)} copy(bf16[8192,64]{0,1:T(8,128)(2,1)} %param.11) | data formatting | bytes 2097152 | tf_op args[4]
  3.3 126.2 %shard_map.86 = (bf16[512,3584]{1,0:T(8,128)(2,1)}, bf16[2,64,128]{2,1,0:T(8,128)(2,1)}) custom-call(s32[2]{0:T(128)} %len_ref.1, bf16[512,3584]{1,0:T(8,128)(2,1)} %hid.1, bf16[512,1024]{1,0:T(8,128)(2,1)} %cot.1, bf16[3584,4096]{1,0:T(8,128)(2,1)} %w.1, bf16[3584,128]{1,0:T(8,128)(2,1)} %pin.1, bf16[8192,64]{1,0:T(8,128)(2,1)} %copy.9.pout), custom_call_target="tpu_custom_call" | custom-call | tf_op jit(solution)/shard_map/pallas_call | solution.py:352
  129.5 2.8 %fusion = f32[2,128]{1,0:T(2,128)} fusion(bf16[128,8192]{1,0:T(8,128)(2,1)} %param.12, bf16[1,2,64,128]{3,2,1,0:T(8,128)(2,1)} %bitcast.5), kind=kOutput, calls=%fused_computation | convolution fusion | flops 4194304 | bytes 2130944 | tf_op jit(solution)/shard_map/dot_general | solution.py:379
  132.4 4.1 %copy.16 = bf16[512,3584]{1,0:T(8,128)(2,1)} copy(bf16[512,3584]{1,0:T(8,128)(2,1)} %get-tuple-element.8) | data formatting | bytes 7340032

commit v2 on v1

v2 whole, which is shorter than its diff:
```python
import functools

import jax
import jax.numpy as jnp
from jax import lax
from jax.experimental import pallas as pl
from jax.experimental.pallas import tpu as pltpu
from jax.sharding import PartitionSpec as P

K_IN = 128
K_OUT = 64
SEQ = 256
TILES = 7
CHUNK = 1024


def kernel(
    F, snake,
    len_ref, hid, cot, w, pin, pout, vp, out, scores,
    X, W, acc, inc, stage, own, po, pi, act, part, rA, gR, G, vbuf,
    ld_sem, w_sem, sib_send, sib_recv, ring_send, ring_recv,
    rs_send, rs_recv, gs_send, gs_recv, ex_send, ex_recv, out_sem, vp_sem,
):
    f = lax.axis_index("fsdp")
    c = lax.axis_index("dp")
    H = F // 2
    T, Dl = own.shape
    FFl = acc.shape[2]
    Tc = T // F
    tile = FFl // TILES

    if snake:
        y, z = lax.rem(f, 2), f // 2
        p = (1 - y) * z + y * (F - 1 - z)

        def at(q):
            h = q // H
            return (1 - h) * (2 * q) + h * (2 * F - 1 - 2 * q)
    else:
        p = f

        def at(q):
            return q

    targets = (at(lax.rem(p + 1, F)), at(lax.rem(p + F - 1, F)))

    def source(d, s):
        q = lax.rem(p - s + F, F) if d == 0 else lax.rem(p + s, F)
        src = at(q)
        half = src // H
        return src - half * H, 1 - (half + c - 2 * half * c)

    def rows(k):
        return pl.ds(k * SEQ, SEQ)

    def ring(slot, d, k):
        i = slot * 4 + d * 2 + k
        return pltpu.make_async_remote_copy(
            src_ref=X.at[slot, d, rows(k)],
            dst_ref=X.at[slot, d, rows(k)],
            send_sem=ring_send.at[i],
            recv_sem=ring_recv.at[i],
            device_id={"fsdp": targets[d]},
            device_id_type=pl.DeviceIdType.MESH,
        )

    def columns(i):
        return pl.ds(pl.multiple_of(i * tile, tile), tile)

    def exchange(d, i):
        return pltpu.make_async_remote_copy(
            src_ref=acc.at[d, :, columns(i)],
            dst_ref=inc.at[:, columns(i)],
            send_sem=ex_send.at[i],
            recv_sem=ex_recv.at[i],
            device_id={"dp": 1 - c},
            device_id_type=pl.DeviceIdType.MESH,
        )

    my_half = f // H
    my_slot = f - my_half * H

    def sibling(d, k):
        return pltpu.make_async_remote_copy(
            src_ref=own.at[rows(k)],
            dst_ref=X.at[my_slot, d, rows(k)],
            send_sem=sib_send.at[k],
            recv_sem=sib_recv.at[k],
            device_id={"dp": 1 - c},
            device_id_type=pl.DeviceIdType.MESH,
        )

    load_cot = pltpu.make_async_copy(cot, own, ld_sem.at[0])
    load_cot.start()
    load_po = pltpu.make_async_copy(
        pout.at[:, pl.ds(pl.multiple_of(f * Dl, Dl), Dl)], po, ld_sem.at[1]
    )
    load_po.start()
    load_pi = pltpu.make_async_copy(pin, pi, ld_sem.at[2])
    load_pi.start()

    def load_hid(h):
        return pltpu.make_async_copy(
            hid.at[:, pl.ds(h * tile, tile)], stage.at[h % 2], ld_sem.at[3 + h % 2]
        )

    load_hid(0).start()
    load_hid(1).start()

    def load_w(i):
        return pltpu.make_async_copy(w.at[:, pl.ds(i * Dl, Dl)], W.at[i], w_sem.at[i])

    def load_vp(q):
        return pltpu.make_async_copy(
            vp.at[:, pl.ds(q * CHUNK, CHUNK)], vbuf.at[q % 2], vp_sem.at[q % 2]
        )

    barrier = pltpu.get_barrier_semaphore()

    @pl.loop(1, F)
    def _(j):
        pl.semaphore_signal(
            barrier, inc=1, device_id={"fsdp": lax.rem(f + j, F)},
            device_id_type=pl.DeviceIdType.MESH,
        )

    pl.semaphore_signal(
        barrier, inc=1, device_id={"dp": 1 - c}, device_id_type=pl.DeviceIdType.MESH
    )

    load_cot.wait()
    for i in range(H):
        load_w(i).start()
    mine = my_half == c
    for k in range(2):
        position = lax.broadcasted_iota(jnp.int32, (SEQ, Dl), 0)
        block = own[rows(k), :]
        masked = jnp.where(position < len_ref[k], block.astype(jnp.float32), 0.0)
        own[rows(k), :] = masked.astype(block.dtype)
    pl.semaphore_wait(barrier, F)

    @pl.when(my_half != c)
    def _():
        for k in range(2):
            for d in range(2):
                @pl.when(c == d)
                def _():
                    sibling(d, k).start()

    @pl.when(mine)
    def _():
        for k in range(2):
            X[my_slot, c, rows(k), :] = own[rows(k), :]
        for d in range(2):
            @pl.when(c == d)
            def _():
                for k in range(2):
                    ring(my_slot, d, k).start()
        for d in range(2):
            @pl.when(c != d)
            def _():
                for k in range(2):
                    sibling(d, k).wait_recv()
                    ring(my_slot, d, k).start()

    @pl.loop(0, T // 8)
    def _(i):
        r = pl.ds(pl.multiple_of(i * 8, 8), 8)
        for d in range(2):
            acc[d, r, :] = jnp.zeros((8, FFl), jnp.float32)

    def project_out():
        load_po.wait()
        for k in range(2):
            o = lax.dot_general(
                own[rows(k), :], po[...], (((1,), (1,)), ((), ())),
                preferred_element_type=jnp.float32,
            )
            for j in range(SEQ // Tc):
                first = o[j * Tc : j * Tc + Tc // 2]
                second = o[j * Tc + Tc // 2 : (j + 1) * Tc]
                run = k * (SEQ // Tc) + j
                part[run, Tc : Tc + Tc // 2, 0:K_OUT] = first
                part[run, Tc : Tc + Tc // 2, K_OUT : 2 * K_OUT] = second

    def project_in(start, stop):
        for h in range(start, stop):
            load_hid(h).wait()
            a = jnp.dot(
                stage[h % 2], pi[h * tile : (h + 1) * tile, :],
                preferred_element_type=jnp.float32,
            )
            act[...] = a if h == 0 else act[...] + a
            if h + 2 < TILES:
                load_hid(h + 2).start()

    def scatter(t, src, dst):
        return pltpu.make_async_remote_copy(
            src_ref=part.at[src], dst_ref=rA.at[dst],
            send_sem=rs_send.at[t], recv_sem=rs_recv.at[dst],
            device_id={"fsdp": t}, device_id_type=pl.DeviceIdType.MESH,
        )

    def spread(t, dst):
        return pltpu.make_async_remote_copy(
            src_ref=gR.at[f], dst_ref=gR.at[dst],
            send_sem=gs_send.at[t], recv_sem=gs_recv.at[dst],
            device_id={"fsdp": t}, device_id_type=pl.DeviceIdType.MESH,
        )

    def scatter_acts():
        for j in range(F):
            part[j, 0:Tc, :] = act[j * Tc : (j + 1) * Tc, :]
        for q in range(2):
            load_vp(q).start()

        @pl.loop(1, F)
        def _(j):
            t = lax.rem(f + j, F)
            scatter(t, t, f).start()

    def reduce_acts():
        def add(j, total):
            t = lax.rem(f + j, F)
            scatter(t, t, t).wait_recv()
            return total + rA[t]

        total = lax.fori_loop(1, F, add, part[f])
        tn = (((0,), (0,)), ((), ()))
        g = jnp.zeros((K_OUT, K_IN), jnp.float32)
        for u in range(2):
            g = g + lax.dot_general(
                total[Tc : Tc + Tc // 2, u * K_OUT : (u + 1) * K_OUT],
                total[u * (Tc // 2) : (u + 1) * (Tc // 2), :],
                tn, precision=lax.Precision.HIGHEST,
                preferred_element_type=jnp.float32,
            )
        gR[f] = g

        @pl.loop(1, F)
        def _(j):
            t = lax.rem(f + j, F)
            spread(t, f).start()

    def reduce_grads():
        @pl.loop(1, F)
        def _(j):
            t = lax.rem(f + j, F)
            spread(t, t).wait_recv()

        for e in range(2):
            g = gR[e * H]
            for t in range(1, H):
                g = g + gR[e * H + t]
            G[e] = g
        total = jnp.zeros(scores.shape, jnp.float32)
        for q in range(K_OUT * K_IN // CHUNK):
            load_vp(q).wait()
            per = CHUNK // K_IN
            low = jnp.concatenate(
                [G[:, q * per + u, :] for u in range(per)], axis=1
            ).astype(jnp.bfloat16)
            total = total + lax.dot_general(
                low, vbuf[q % 2], (((1,), (1,)), ((), ())),
                preferred_element_type=jnp.float32,
            )
            if q + 2 < K_OUT * K_IN // CHUNK:
                load_vp(q + 2).start()
        scores[...] = total

    def product(slot, d, last):
        @pl.loop(0, TILES)
        def _(i):
            n = columns(i)
            acc[d, :, n] += lax.dot_general(
                X[slot, d], W[slot, n, :], (((1,), (1,)), ((), ())),
                preferred_element_type=jnp.float32,
            )

            @pl.when((last == 1) & (c != d))
            def _():
                exchange(d, i).start()

    def forward(s, d, k):
        slot, live = source(d, s)

        @pl.when(live == 1)
        def _():
            ring(slot, d, k).wait_recv()

            @pl.when(s < F - 1)
            def _():
                ring(slot, d, k).start()

    def final(count):
        return 1 - jnp.minimum(H - count, 1)

    def step(s, seen):
        counts = []
        for d in range(2):
            for e in range(2):
                forward(s, e, d)

            if d == 0:
                @pl.when(s == 1)
                def _():
                    load_pi.wait()
                    project_out()
                    project_in(0, 3)

                @pl.when(s == 2)
                def _():
                    for i in range(H):
                        load_w(i).wait()
            else:
                @pl.when(s == 1)
                def _():
                    project_in(3, TILES)
                    scatter_acts()

            @pl.when((s == 2) & mine)
            def _():
                product(my_slot, d, 0)

            slot, live = source(d, s - 1)
            counts.append(seen[d] + live)

            @pl.when((live == 1) & (s >= 2))
            def _():
                product(slot, d, final(counts[d]))

        @pl.when(s == 4)
        def _():
            reduce_acts()

        @pl.when(s == 6)
        def _():
            reduce_grads()

        return tuple(counts)

    seen = lax.fori_loop(1, F, step, (0, 0))
    for other in (True, False):
        for d in range(2):
            slot, live = source(d, F - 1)

            @pl.when((live == 1) & ((c != d) if other else (c == d)))
            def _():
                product(slot, d, final(seen[d] + live))

    def write(b):
        return pltpu.make_async_copy(
            stage.at[b % 2], out.at[:, pl.ds(b * tile, tile)], out_sem.at[b % 2]
        )

    for b in range(TILES):
        exchange(0, b).wait_recv()
        if b >= 2:
            write(b - 2).wait()

        @pl.loop(0, T // 16)
        def _(i):
            r = pl.ds(pl.multiple_of(i * 16, 16), 16)
            n = slice(b * tile, (b + 1) * tile)
            stage[b % 2, r, :] = (acc[c, r, n] + inc[r, n]).astype(stage.dtype)

        write(b).start()

    for b in range(TILES - 2, TILES):
        write(b).wait()

    @pl.when(my_half != c)
    def _():
        for k in range(2):
            sibling(0, k).wait_send()

    for i in range(TILES):
        exchange(0, i).wait_send()

    @pl.loop(1, F)
    def _(j):
        t = lax.rem(f + j, F)
        scatter(t, t, f).wait_send()
        spread(t, f).wait_send()

    @pl.loop(0, F - 1)
    def _(s):
        for d in range(2):
            slot, act = source(d, s)

            @pl.when(act == 1)
            def _():
                for k in range(2):
                    ring(slot, d, k).wait_send()


def per_device(F, hidden, cotangent, down_weight, proj_in, proj_out, valid_proj, lengths):
    T, FFl = hidden.shape
    Dl = cotangent.shape[1]
    H = F // 2
    Tc = T // F
    any_spec = pl.BlockSpec(memory_space=pl.ANY)
    vmem = pl.BlockSpec(memory_space=pltpu.VMEM)
    dma = pltpu.SemaphoreType.DMA
    V = valid_proj.shape[0]
    return pl.pallas_call(
        functools.partial(kernel, F, F == 8),
        out_shape=(
            jax.ShapeDtypeStruct((T, FFl), jnp.bfloat16),
            jax.ShapeDtypeStruct((T // SEQ, V), jnp.float32),
        ),
        in_specs=[pl.BlockSpec(memory_space=pltpu.SMEM)] + [any_spec] * 6,
        out_specs=(any_spec, vmem),
        scratch_shapes=[
            pltpu.VMEM((H, 2, T, Dl), jnp.bfloat16),
            pltpu.VMEM((H, FFl, Dl), jnp.bfloat16),
            pltpu.VMEM((2, T, FFl), jnp.float32),
            pltpu.VMEM((T, FFl), jnp.float32),
            pltpu.VMEM((2, T, FFl // TILES), jnp.bfloat16),
            pltpu.VMEM((T, Dl), jnp.bfloat16),
            pltpu.VMEM((K_OUT, Dl), jnp.bfloat16),
            pltpu.VMEM((FFl, K_IN), jnp.bfloat16),
            pltpu.VMEM((T, K_IN), jnp.float32),
            pltpu.VMEM((F, Tc + Tc // 2, K_IN), jnp.float32),
            pltpu.VMEM((F, Tc + Tc // 2, K_IN), jnp.float32),
            pltpu.VMEM((F, K_OUT, K_IN), jnp.float32),
            pltpu.VMEM((T // SEQ, K_OUT, K_IN), jnp.float32),
            pltpu.VMEM((2, V, CHUNK), jnp.bfloat16),
            dma((5,)), dma((H,)), dma((2,)), dma((2,)), dma((4 * H,)), dma((4 * H,)),
            dma((F,)), dma((F,)), dma((F,)), dma((F,)), dma((TILES,)), dma((TILES,)),
            dma((2,)), dma((2,)),
        ],
        compiler_params=pltpu.CompilerParams(
            collective_id=0, has_side_effects=True, vmem_limit_bytes=66584576
        ),
    )(lengths, hidden, cotangent, down_weight, proj_in, proj_out.T, valid_proj)


def solution(mesh):
    in_specs = (
        P(("group", "dp"), "fsdp"),
        P(("group", "dp"), "fsdp"),
        P("fsdp", "dp"),
        P("fsdp", None),
        P(),
        P(("group", "fsdp"), None),
        P(("group", "dp")),
    )
    out_specs = (P(("group", "dp"), "fsdp"), P(("group", "dp"), "fsdp"))
    return jax.shard_map(
        functools.partial(per_device, mesh.shape["fsdp"]),
        mesh=mesh, in_specs=in_specs, out_specs=out_specs, check_vma=False,
    )
```

time: 137 us -> 131 us (0.956)
  matrix products: 2.83 us -> 0 us
  local copies, waits for them, and re-layouts: 6.83 us -> 4.68 us
    dot_general x1 -> x0, matrix products: 2.83 us -> none  [per_device(): lax.dot_general(grads_low.reshape(2, K_OUT * K_IN), valid_proj, (((1,), (...]
    unnamed x2 -> x4, local copies, waits for them, and re-layouts: 6.83 us -> 4.68 us
where the time goes in v2:
time: 131 us
  Pallas kernels  126 us (96%)
  local copies, waits for them, and re-layouts  4.68 us (4%)
    pallas_call x1, Pallas kernels, per_device(): pl.pallas_call(functools.partial(kernel, F, F == 8), out_shape=(jax.Shape...  126 us
    unnamed x4, local copies, waits for them, and re-layouts  4.68 us

profile of v2, /device:TPU:19, one launch (start us, length us, event | category | flops | bytes accessed | tf_op | source)
XLA Modules:
  0.0 131.0 jit_solution(190100371706860985)
XLA Ops:
  0.6 125.7 %shard_map.86 = (bf16[512,3584]{1,0:T(8,128)(2,1)}, f32[2,128]{1,0:T(2,128)}) custom-call(s32[2]{0:T(128)} %len_ref.1, bf16[512,3584]{1,0:T(8,128)(2,1)} %hid.1, bf16[512,1024]{1,0:T(8,128)(2,1)} %cot.1, bf16[3584,4096]{1,0:T(8,128)(2,1)} %w.1, bf16[3584,128]{1,0:T(8,128)(2,1)} %pin.1, bf16[64,8192]{1,0:T(8,128)(2,1)} %bitcast.1, bf16[128,8192]{1,0:T(8,128)(2,1)} %vp.1), custom_call_target="tpu_custom_call" | custom-call | tf_op jit(solution)/shard_map/pallas_call | solution.py:406
  126.4 0.0 copy-start
  126.4 4.1 %copy.11 = bf16[512,3584]{1,0:T(8,128)(2,1)} copy(bf16[512,3584]{1,0:T(8,128)(2,1)} %get-tuple-element.4) | data formatting | bytes 7340032
  130.5 0.0 copy-done
  130.5 0.6 copy.12
Async XLA Ops:
  126.4 4.1 %copy-start = (f32[2,128]{1,0:T(2,128)S(1)}, f32[2,128]{1,0:T(2,128)}, u32[]{:S(2)}) copy-start(f32[2,128]{1,0:T(2,128)} %get-tuple-element.5) | copy-start | bytes 3076

commit v3 on v2

--- a/solution.py
+++ b/solution.py
@@ -54,10 +54,11 @@
         return pl.ds(k * SEQ, SEQ)
 
     def ring(slot, d, k):
-        i = slot * 4 + d * 2 + k
+        i = slot * 8 + d * 4 + k
+        quarter = pl.ds(k * (SEQ // 2), SEQ // 2)
         return pltpu.make_async_remote_copy(
-            src_ref=X.at[slot, d, rows(k)],
-            dst_ref=X.at[slot, d, rows(k)],
+            src_ref=X.at[slot, d, quarter],
+            dst_ref=X.at[slot, d, quarter],
             send_sem=ring_send.at[i],
             recv_sem=ring_recv.at[i],
             device_id={"fsdp": targets[d]},
@@ -154,14 +155,15 @@
         for d in range(2):
             @pl.when(c == d)
             def _():
-                for k in range(2):
+                for k in range(4):
                     ring(my_slot, d, k).start()
         for d in range(2):
             @pl.when(c != d)
             def _():
                 for k in range(2):
                     sibling(d, k).wait_recv()
-                    ring(my_slot, d, k).start()
+                    ring(my_slot, d, 2 * k).start()
+                    ring(my_slot, d, 2 * k + 1).start()
 
     @pl.loop(0, T // 8)
     def _(i):
@@ -268,8 +270,8 @@
                 load_vp(q + 2).start()
         scores[...] = total
 
-    def product(slot, d, last):
-        @pl.loop(0, TILES)
+    def product(slot, d, last, start=0, stop=TILES):
+        @pl.loop(start, stop)
         def _(i):
             n = columns(i)
             acc[d, :, n] += lax.dot_general(
@@ -299,7 +301,7 @@
         counts = []
         for d in range(2):
             for e in range(2):
-                forward(s, e, d)
+                forward(s, e, 2 * d)
 
             if d == 0:
                 @pl.when(s == 1)
@@ -327,7 +329,14 @@
 
             @pl.when((live == 1) & (s >= 2))
             def _():
-                product(slot, d, final(counts[d]))
+                product(slot, d, final(counts[d]), 0, TILES // 2)
+
+            for e in range(2):
+                forward(s, e, 2 * d + 1)
+
+            @pl.when((live == 1) & (s >= 2))
+            def _():
+                product(slot, d, final(counts[d]), TILES // 2, TILES)
 
         @pl.when(s == 4)
         def _():
@@ -390,7 +399,7 @@
 
             @pl.when(act == 1)
             def _():
-                for k in range(2):
+                for k in range(4):
                     ring(slot, d, k).wait_send()
 
 
@@ -426,7 +435,7 @@
             pltpu.VMEM((F, K_OUT, K_IN), jnp.float32),
             pltpu.VMEM((T // SEQ, K_OUT, K_IN), jnp.float32),
             pltpu.VMEM((2, V, CHUNK), jnp.bfloat16),
-            dma((5,)), dma((H,)), dma((2,)), dma((2,)), dma((4 * H,)), dma((4 * H,)),
+            dma((5,)), dma((H,)), dma((2,)), dma((2,)), dma((8 * H,)), dma((8 * H,)),
             dma((F,)), dma((F,)), dma((F,)), dma((F,)), dma((TILES,)), dma((TILES,)),
             dma((2,)), dma((2,)),
         ],

time: 131 us -> 125 us (0.954)
  the two profiles are of different devices: /device:TPU:19 before, /device:TPU:0 now
where the time goes in v3:
time: 125 us
  Pallas kernels  119 us (95%)
  local copies, waits for them, and re-layouts  4.68 us (4%)
    pallas_call x1, Pallas kernels, per_device(): pl.pallas_call(functools.partial(kernel, F, F == 8), out_shape=(jax.Shape...  119 us
    unnamed x4, local copies, waits for them, and re-layouts  4.68 us

profile of v3, /device:TPU:0, one launch (start us, length us, event | category | flops | bytes accessed | tf_op | source)
XLA Modules:
  0.0 124.7 jit_solution(6098812213342655043)
XLA Ops:
  0.6 119.3 %shard_map.86 = (bf16[512,3584]{1,0:T(8,128)(2,1)}, f32[2,128]{1,0:T(2,128)}) custom-call(s32[2]{0:T(128)} %len_ref.1, bf16[512,3584]{1,0:T(8,128)(2,1)} %hid.1, bf16[512,1024]{1,0:T(8,128)(2,1)} %cot.1, bf16[3584,4096]{1,0:T(8,128)(2,1)} %w.1, bf16[3584,128]{1,0:T(8,128)(2,1)} %pin.1, bf16[64,8192]{1,0:T(8,128)(2,1)} %bitcast.1, bf16[128,8192]{1,0:T(8,128)(2,1)} %vp.1), custom_call_target="tpu_custom_call" | custom-call | tf_op jit(solution)/shard_map/pallas_call | solution.py:415
  120.0 0.0 copy-start
  120.0 4.1 %copy.11 = bf16[512,3584]{1,0:T(8,128)(2,1)} copy(bf16[512,3584]{1,0:T(8,128)(2,1)} %get-tuple-element.4) | data formatting | bytes 7340032
  124.1 0.0 copy-done
  124.1 0.6 copy.12
Async XLA Ops:
  120.0 4.1 %copy-start = (f32[2,128]{1,0:T(2,128)S(1)}, f32[2,128]{1,0:T(2,128)}, u32[]{:S(2)}) copy-start(f32[2,128]{1,0:T(2,128)} %get-tuple-element.5) | copy-start | bytes 3076
